TPU v7x, 128 devices: a whole 4x4x4 slice. The times are simulated.
128 devices in a mesh: dp: 4 (over y), context: 16 (over x, z), tensor: 2 (over core).
Axes of the slice: x: 4, y: 4, z: 4, core: 2. Of those that a mesh axis runs over, the one named last changes fastest.
Arguments:
- tokens: bfloat16 [4, 8192, 2048], P('dp', 'context'), may hold values from -6 to 6
- cotangent: bfloat16 [4, 8192, 2048], P('dp', 'context'), may hold values from -6 to 6
- query_weight: bfloat16 [2048, 2048], P('dp', 'tensor'), may hold values from -0.125 to 0.125
- key_master: float32 [2048, 2048], P('dp', 'tensor'), may hold values from -0.125 to 0.125
- value_weight: bfloat16 [2048, 2048], P('dp', 'tensor'), may hold values from -0.125 to 0.125
- out_weight: bfloat16 [2048, 2048], P('dp', 'tensor'), may hold values from -0.125 to 0.125
- key_moment: float32 [2048, 2048], P('dp', 'tensor'), may hold values from -6 to 6
- key_second: float32 [2048, 2048], P('dp', 'tensor'), may hold values from 0.65536 to 6.5536
Outputs:
- input_grad: bfloat16 [4, 8192, 2048], P('dp', 'context', 'tensor')
- key_master_new: float32 [2048, 2048], P('dp', 'tensor')
- key_moment_new: float32 [2048, 2048], P('dp', 'tensor')
- key_second_new: float32 [2048, 2048], P('dp', 'tensor')
All inputs are finite; a program needn't handle non-finite values.
Results may differ from a plain program's by a relative error of at most 0.012.
The roundings to bfloat16 on the way count: a program that leaves them out, or rounds other values in their place, can miss the bound.
Values may be sent and summed in bfloat16 or wider, within the bound.
No kernel may reach another device: no remote copies, remote signals or barrier semaphores. Data moves between devices by JAX's collectives and lax.ppermute only.
A program may use at most 128 MiB of HBM per device.

v0:
```python
import jax
import jax.numpy as jnp
from jax import lax
from jax.sharding import PartitionSpec as P

HEAD = 128


norm_eps = 1e-06
beta_one = 0.9
beta_two = 0.999
bias_one = 0.9999734386011124
bias_two = 0.09520785288
adam_eps = 1e-08
learn_rate = 0.001
weight_decay = 0.1


def adam_update(master, moment, second, gradient):
    moment_new = beta_one * moment + (1.0 - beta_one) * gradient
    second_new = beta_two * second + (1.0 - beta_two) * gradient * gradient
    update = moment_new / bias_one / (jnp.sqrt(second_new / bias_two) + adam_eps)
    master_new = master - learn_rate * (update + weight_decay * master)
    return (master_new, moment_new, second_new)


def contract_last(left, right):
    return lax.dot_general(
        left, right, (((1,), (1,)), ((), ())), preferred_element_type=jnp.float32
    )


def local(
    tokens, cotangent, query_weight, key_master, value_weight, out_weight, key_moment, key_second
):
    token_count = tokens.shape[1]
    model_width = tokens.shape[2]
    flat_tokens = tokens.reshape(token_count, model_width)
    flat_cotangent = cotangent.reshape(token_count, model_width)
    replicas = lax.axis_size("dp")
    query_full, key_full, value_full, out_full = (
        lax.all_gather(query_weight, "dp", axis=0, tiled=True),
        lax.all_gather(key_master.astype(jnp.bfloat16), "dp", axis=0, tiled=True),
        lax.all_gather(value_weight, "dp", axis=0, tiled=True),
        lax.all_gather(out_weight, "dp", axis=0, tiled=True),
    )
    column_count = query_full.shape[1]
    head_count = column_count // HEAD

    def project(weight):
        product = jnp.dot(flat_tokens, weight, preferred_element_type=jnp.float32)
        return product.astype(jnp.bfloat16).reshape(token_count, head_count, HEAD)

    queries = project(query_full)
    key_rows = project(key_full)
    value_rows = project(value_full)
    local_memory = jnp.einsum(
        "shd,she->hde", key_rows, value_rows, preferred_element_type=jnp.float32
    )
    memory = lax.psum(local_memory, "context")
    memory_b = memory.astype(jnp.bfloat16)
    attended = jnp.einsum("shd,hde->she", queries, memory_b, preferred_element_type=jnp.float32)
    root_mean = jnp.sqrt(jnp.mean(attended * attended, axis=-1, keepdims=True) + norm_eps)
    normed = attended / root_mean
    grad_normed = jnp.dot(flat_cotangent, out_full, preferred_element_type=jnp.float32).reshape(
        token_count, head_count, HEAD
    )
    inner = jnp.mean(grad_normed * normed, axis=-1, keepdims=True)
    grad_attended = ((grad_normed - normed * inner) / root_mean).astype(jnp.bfloat16)
    local_grad_memory = jnp.einsum(
        "shd,she->hde", queries, grad_attended, preferred_element_type=jnp.float32
    )
    grad_memory = lax.psum(local_grad_memory, "context")
    grad_memory_b = grad_memory.astype(jnp.bfloat16)
    grad_queries = jnp.einsum(
        "she,hde->shd", grad_attended, memory_b, preferred_element_type=jnp.float32
    )
    grad_queries = grad_queries.astype(jnp.bfloat16).reshape(token_count, column_count)
    grad_keys = jnp.einsum(
        "she,hde->shd", value_rows, grad_memory_b, preferred_element_type=jnp.float32
    )
    grad_keys = grad_keys.astype(jnp.bfloat16).reshape(token_count, column_count)
    grad_values = jnp.einsum(
        "shd,hde->she", key_rows, grad_memory_b, preferred_element_type=jnp.float32
    )
    grad_values = grad_values.astype(jnp.bfloat16).reshape(token_count, column_count)
    input_terms = contract_last(grad_queries, query_full) + contract_last(grad_keys, key_full)
    input_terms = input_terms + contract_last(grad_values, value_full)
    input_grad = lax.psum_scatter(input_terms, "tensor", scatter_dimension=1, tiled=True).astype(
        jnp.bfloat16
    )
    input_grad = input_grad.reshape(1, token_count, input_grad.shape[1])
    scale_factor = 1.0 / replicas
    shard_rows = key_master.shape[0]
    product = lax.dot_general(
        flat_tokens, grad_keys, (((0,), (0,)), ((), ())), preferred_element_type=jnp.float32
    )
    whole_grad = lax.psum(product * scale_factor, ("dp", "context"))
    gradient = lax.dynamic_slice_in_dim(
        whole_grad, lax.axis_index("dp") * shard_rows, shard_rows, 0
    )
    master_new, moment_new, second_new = adam_update(key_master, key_moment, key_second, gradient)
    return (input_grad, master_new, moment_new, second_new)


def solution(mesh):
    return jax.shard_map(
        local,
        mesh=mesh,
        in_specs=(
            P("dp", "context", None),
            P("dp", "context", None),
            P("dp", "tensor"),
            P("dp", "tensor"),
            P("dp", "tensor"),
            P("dp", "tensor"),
            P("dp", "tensor"),
            P("dp", "tensor"),
        ),
        out_specs=(
            P("dp", "context", "tensor"),
            P("dp", "tensor"),
            P("dp", "tensor"),
            P("dp", "tensor"),
        ),
        check_vma=False,
    )
```

profile of v0, /device:TPU:2, one launch (start us, length us, event | category | flops | bytes accessed | tf_op | source)
XLA Modules:
  0.0 541.4 jit_solution(17497407811575384133)
XLA Ops:
  7.2 0.0 all-gather.5.cloned.1.call-start
  7.2 2.9 convert_element_type.42
  10.1 0.0 all-gather.7.cloned.1.call-start
  10.2 0.7 all-gather.7.cloned.1.call-update
  10.9 0.0 all-gather.11.cloned.1.call-start
  10.9 0.7 all-gather.11.cloned.1.call-update
  11.6 0.0 all-gather.9.cloned.1.call-start
  11.7 0.5 all-gather.9.cloned.1.call-update
  12.2 0.0 all-reduce.4.cloned.1.call-start
  12.2 48.7 %all-gather.5.cloned.1.call-done = bf16[2048,1024]{1,0:T(8,128)(2,1)} async-done(((bf16[512,1024]{1,0:T(8,128)(2,1)}), bf16[2048,1024]{1,0:T(8,128)(2,1)}) %all-gather.5.cloned.1.call-update) | async-done | bytes 4194320 | tf_op jit(solution)/shard_map/all_gather | solution.py:43
  60.9 4.5 fusion.23
  65.5 45.8 %all-gather.7.cloned.1.call-done = bf16[2048,1024]{1,0:T(8,128)(2,1)} async-done(((bf16[512,1024]{1,0:T(8,128)(2,1)}), bf16[2048,1024]{1,0:T(8,128)(2,1)}) %all-gather.7.cloned.1.call-update) | async-done | bytes 4194320 | tf_op jit(solution)/shard_map/all_gather | solution.py:44
  111.2 4.5 fusion.20
  115.8 1.0 copy-done.12
  116.7 1.4 fusion.27
  118.1 43.4 %all-gather.11.cloned.1.call-done = bf16[2048,1024]{1,0:T(8,128)(2,1)} async-done(((bf16[512,1024]{1,0:T(8,128)(2,1)}), bf16[2048,1024]{1,0:T(8,128)(2,1)}) %all-gather.11.cloned.1.call-update) | async-done | bytes 4194320 | tf_op jit(solution)/shard_map/all_gather | solution.py:42
  161.5 5.5 %fusion.17 = bf16[512,1024]{1,0:T(8,128)(2,1)} fusion(bf16[2048,1024]{1,0:T(8,128)(2,1)} %all-gather.11.cloned.1.call-done, bf16[1,512,2048]{2,1,0:T(8,128)(2,1)S(1)} %copy-done), kind=kOutput, calls=%fused_computation.25 | convolution fusion | flops 2148007936 | bytes 7340032 | tf_op jit(solution)/shard_map/dot_general | solution.py:51
  167.0 1.5 copy.34
  168.5 74.7 %all-reduce.5 = bf16[8,128,128]{2,1,0:T(8,128)(2,1)S(1)} all-reduce(f32[8,128,128]{2,1,0:T(8,128)} %fusion.27), channel_id=1, replica_groups=mesh['dp'=4,'context'=16,'tensor'=2] {'context'}, use_global_device_ids=true, to_apply=%region_0.0 | all-reduce | flops 131072 | bytes 786432 | tf_op jit(solution)/shard_map/psum | solution.py:60
  243.3 1.8 fusion.1
  245.1 6.6 %copy.14 = bf16[1024,2048]{1,0:T(8,128)(2,1)} copy(bf16[1024,2048]{0,1:T(8,128)(2,1)} %bitcast.85) | data formatting | bytes 8388608 | tf_op jit(solution)/shard_map/dot_general | solution.py:65
  251.7 6.0 %multiply_reduce_fusion = (f32[512,8]{0,1:T(8,128)S(1)}, f32[512,8,128]{0,2,1:T(8,128)S(1)}) fusion(f32[512,8]{0,1:T(8,128)S(1)} %add_sqrt_fusion, f32[8,128,512]{2,1,0:T(8,128)} %get-tuple-element.12, bf16[8,128,2048]{2,1,0:T(8,128)(2,1)} %bitcast.86, bf16[1,512,2048]{2,1,0:T(8,128)(2,1)} %param.9), kind=kOutput, calls=%fused_computation.19 | convolution fusion | flops 2149052416 | bytes 10518528 | tf_op jit(solution)/shard_map/dot_general | solution.py:65
  257.7 0.6 divide_convert_fusion
  258.3 0.6 copy-done.3
  258.9 1.2 fusion.42
  260.1 75.8 %all-reduce.6 = bf16[8,128,128]{2,1,0:T(8,128)(2,1)S(1)} all-reduce(f32[8,128,128]{2,1,0:T(8,128)} %fusion.42), channel_id=1, replica_groups=mesh['dp'=4,'context'=16,'tensor'=2] {'context'}, use_global_device_ids=true, to_apply=%region_3.0 | all-reduce | flops 131072 | bytes 786432 | tf_op jit(solution)/shard_map/psum | solution.py:73
  335.9 1.7 convolution_convert_fusion.1
  337.6 1.0 copy-done.13
  338.6 5.6 %multiply_bitcast_fusion = f32[2048,1024]{0,1:T(8,128)} fusion(bf16[512,1024]{0,1:T(8,128)(2,1)S(1)} %bitcast.87, bf16[1,512,2048]{2,1,0:T(8,128)(2,1)S(1)} %copy-done), kind=kOutput, calls=%fused_computation | convolution fusion | flops 2149580800 | bytes 11534336 | tf_op jit(solution)/shard_map/dot_general | solution.py:95
  344.2 0.0 reduce-scatter.2.cloned.1.call-start
  344.3 0.9 copy-done.9
  345.1 0.4 convolution_convert_fusion.2
  345.5 0.5 convolution_convert_fusion
  346.0 0.4 copy-done.14
  346.4 4.7 fusion.43
  351.2 2.4 fusion.41
  353.6 4.4 add_add_fusion
  358.0 1.6 copy-done.4
  359.5 1.8 copy.26
  361.3 2.9 copy.23
  364.3 3.0 copy.24
  367.3 148.8 %all-reduce.4.cloned.1.call-done = f32[2048,1024]{0,1:T(8,128)} async-done(((f32[2048,1024]{0,1:T(8,128)}), f32[2048,1024]{0,1:T(8,128)}) %all-reduce.4.cloned.1.call-update) | async-done | bytes 8388624 | tf_op jit(solution)/shard_map/psum | solution.py:98
  516.1 6.7 %multiply_subtract_fusion = (f32[512,1024]{0,1:T(8,128)}, f32[512,1024]{0,1:T(8,128)}, f32[512,1024]{0,1:T(8,128)}) fusion(f32[512,1024]{0,1:T(8,128)S(1)} %copy-done.6, f32[2048,1024]{0,1:T(8,128)} %all-reduce.4.cloned.1.call-done, s32[]{:T(128)S(6)} %select_n.3, f32[512,1024]{0,1:T(8,128)} %copy.23, f32[512,1024]{0,1:T(8,128)} %copy.24), kind=kLoop, calls=%fused_computation.16 | loop fusion | flops 7864320 | bytes 14680068 | tf_op jit(solution)/shard_map/sub | solution.py:23
  522.8 3.0 copy.27
  525.8 1.8 copy.28
  527.6 3.6 copy.29
  531.2 0.6 reduce-scatter.2.cloned.1.call-done
  531.8 2.7 convert_bitcast_fusion
  (34 shorter events, 0.2 us)
Async XLA Ops:
  7.2 53.8 %copy-start = (bf16[1,512,2048]{2,1,0:T(8,128)(2,1)S(1)}, bf16[1,512,2048]{2,1,0:T(8,128)(2,1)}, u32[]{:S(2)}) copy-start(bf16[1,512,2048]{2,1,0:T(8,128)(2,1)} %param.8) | copy-start | bytes 6291460
  7.2 53.7 %all-gather.5.cloned.1.call-start = ((), (), s32[]{:S(2)}) async-start(), calls=%async_computation.1 | async-start | bytes 5242880 | tf_op jit(solution)/shard_map/all_gather | solution.py:43
  10.1 101.1 %all-gather.7.cloned.1.call-start = ((), (), s32[]{:S(2)}) async-start(), calls=%async_computation.2 | async-start | bytes 5242880 | tf_op jit(solution)/shard_map/all_gather | solution.py:44
  10.9 150.7 %all-gather.11.cloned.1.call-start = ((), (), s32[]{:S(2)}) async-start(), calls=%async_computation.4 | async-start | bytes 5242880 | tf_op jit(solution)/shard_map/all_gather | solution.py:42
  11.6 233.5 %all-gather.9.cloned.1.call-start = ((), (), s32[]{:S(2)}) async-start(), calls=%async_computation.3 | async-start | bytes 5242880 | tf_op jit(solution)/shard_map/all_gather | solution.py:45
  12.2 503.9 %all-reduce.4.cloned.1.call-start = ((), (), s32[]{:S(2)}) async-start(), calls=%async_computation.6 | async-start | bytes 16777216 | tf_op jit(solution)/shard_map/psum | solution.py:98
  65.5 50.3 %copy-start.10 = (bf16[64,8,8,128]{3,2,1,0:T(8,128)(2,1)}, bf16[64,8,8,128]{3,2,1,0:T(8,128)(2,1)S(1)}, u32[]{:S(2)}) copy-start(bf16[64,8,8,128]{3,2,1,0:T(8,128)(2,1)S(1)} %fusion.23) | copy-start | bytes 3145732
  115.8 1.0 copy-start.12
  168.5 76.5 %copy-start.2 = (bf16[512,1024]{0,1:T(8,128)(2,1)}, bf16[512,1024]{0,1:T(8,128)(2,1)S(1)}, u32[]{:S(2)}) copy-start(bf16[512,1024]{0,1:T(8,128)(2,1)S(1)} %copy.34) | copy-start | bytes 3145732
  243.2 8.4 %copy-start.8 = (bf16[8,128,128]{2,1,0:T(8,128)(2,1)}, bf16[8,128,128]{2,1,0:T(8,128)(2,1)S(1)}, u32[]{:S(2)}) copy-start(bf16[8,128,128]{2,1,0:T(8,128)(2,1)S(1)} %all-reduce.5) | copy-start | bytes 786436
  251.7 6.0 %copy-start.5 = (f32[8,128,512]{2,1,0:T(8,128)S(1)}, f32[8,128,512]{2,1,0:T(8,128)}, u32[]{:S(2)}) copy-start(f32[8,128,512]{2,1,0:T(8,128)} %get-tuple-element.12) | copy-start | bytes 6291460
  257.7 1.2 copy-start.3
  337.6 1.0 copy-start.13
  344.2 0.9 copy-start.9
  344.2 1.3 copy-start.11
  344.2 187.6 %reduce-scatter.2.cloned.1.call-start = ((), (), s32[]{:S(2)}) async-start(), calls=%async_computation.5 | async-start | bytes 6291456 | tf_op jit(solution)/shard_map/reduce_scatter | solution.py:89
  345.1 1.3 copy-start.14
  346.4 4.7 copy-start.16
  351.2 2.4 copy-start.15
  357.9 1.6 copy-start.4
  364.3 151.8 %copy-start.6 = (f32[512,1024]{0,1:T(8,128)S(1)}, f32[512,1024]{0,1:T(8,128)}, u32[]{:S(2)}) copy-start(f32[512,1024]{0,1:T(8,128)} %copy.26) | copy-start | bytes 6291460
  522.8 3.0 copy-start.7
  527.6 6.9 %copy-start.1 = (bf16[1,512,2048]{2,1,0:T(8,128)(2,1)S(1)}, bf16[1,512,2048]{2,1,0:T(8,128)(2,1)}, u32[]{:S(2)}) copy-start(bf16[1,512,2048]{2,1,0:T(8,128)(2,1)} %param.8) | copy-start | bytes 6291460
Sparse Core Ops, SparseCore 0:
  10.3 50.6 all-gather.4
  62.6 48.5 all-gather.6
  112.9 48.5 all-gather.10
  163.1 48.5 all-gather.8
  344.3 171.7 all-reduce.3
  518.4 13.3 reduce-scatter.1
where the time goes:
time: 543 us; the launch traced here: 541 us
  waiting for transfers between devices  289 us (53%)
  blocking collectives  150 us (28%)
  matrix products  44.5 us (8%)
  local copies, waits for them, and re-layouts  29.6 us (5%)
  between operations  14.3 us (3%)
  other arithmetic  13 us (2%)
    psum x1, waiting for transfers between devices, local(): whole_grad = lax.psum(product * scale_factor, ('dp', 'context'))  149 us
    psum x1, blocking collectives, local(): grad_memory = lax.psum(local_grad_memory, 'context')  75.8 us
    psum x1, blocking collectives, local(): memory = lax.psum(local_memory, 'context')  74.7 us
    all_gather x1, waiting for transfers between devices, local(): lax.all_gather(key_master.astype(jnp.bfloat16), 'dp', axis=0, tiled=True)  48.7 us
    all_gather x1, waiting for transfers between devices, local(): lax.all_gather(value_weight, 'dp', axis=0, tiled=True)  45.8 us
    all_gather x1, waiting for transfers between devices, local(): lax.all_gather(query_weight, 'dp', axis=0, tiled=True)  43.4 us
    unnamed x40, local copies, waits for them, and re-layouts  21.5 us
    dot_general x3, matrix products, project(): product = jnp.dot(flat_tokens, weight, preferred_element_type=jnp.float32)  14.5 us
  transfers between devices with their start and end apart: 6, of which 5 were waited for; matrix products, arithmetic and copies ran while one was open for 10% of the time, Pallas kernels for 0%

commit v1 on v0

v1 whole, which is shorter than its diff:
```python
import functools

import jax
import jax.numpy as jnp
from jax import lax
from jax.experimental import pallas as pl
from jax.experimental.pallas import tpu as pltpu
from jax.sharding import PartitionSpec as P

HEAD = 128
BF = jnp.bfloat16
F32 = jnp.float32

norm_eps = 1e-06
beta_one = 0.9
beta_two = 0.999
bias_one = 0.9999734386011124
bias_two = 0.09520785288
adam_eps = 1e-08
learn_rate = 0.001
weight_decay = 0.1

VMEM = pl.BlockSpec(memory_space=pltpu.VMEM)
SMEM = pl.BlockSpec(memory_space=pltpu.SMEM)
CORE = ("context", "tensor")


def y_pairs(shift):
    return [(y, (y + shift) % 4) for y in range(4)]


def plane_target(x, z, core, shift, cross):
    if (core == 0) != cross:
        return ((x + shift) % 4) * 4 + z
    return x * 4 + (z + shift) % 4


def plane_pairs(shift, cross=False):
    return [
        ((x * 4 + z) * 2 + core, plane_target(x, z, core, shift, cross) * 2 + core)
        for x in range(4)
        for z in range(4)
        for core in range(2)
    ]


def plane_groups(cross=False):
    groups = []
    for other in range(4):
        for core in range(2):
            if (core == 0) != cross:
                groups.append([(x * 4 + other) * 2 + core for x in range(4)])
            else:
                groups.append([(other * 4 + z) * 2 + core for z in range(4)])
    return groups


def send_y(block, shift):
    return lax.ppermute(block, "dp", y_pairs(shift))


def send_plane(block, shift, cross=False):
    return lax.ppermute(block, CORE, plane_pairs(shift, cross))


def after(value, *others):
    return lax.optimization_barrier((value,) + others)[0]


def run(kernel, out_shape, args, flops, scalars=True, limit=48):
    specs = [SMEM] + [VMEM] * (len(args) - 1) if scalars else [VMEM] * len(args)
    many = isinstance(out_shape, (list, tuple))
    total = sum(a.size * a.dtype.itemsize for a in args)
    total += sum(o.size * o.dtype.itemsize for o in (out_shape if many else [out_shape]))
    return pl.pallas_call(
        kernel,
        out_shape=out_shape,
        in_specs=specs,
        out_specs=[VMEM] * len(out_shape) if many else VMEM,
        compiler_params=pltpu.CompilerParams(vmem_limit_bytes=limit << 20),
        cost_estimate=pl.CostEstimate(flops=flops, bytes_accessed=total, transcendentals=0),
    )(*args)


def shape(dims, dtype):
    return jax.ShapeDtypeStruct(dims, dtype)


def dot(left, right, left_dim, right_dim):
    return lax.dot_general(
        left, right, (((left_dim,), (right_dim,)), ((), ())), preferred_element_type=F32
    )


def at(index, size):
    return pl.ds(pl.multiple_of(index * size, size), size)


def gather_y(own, place):
    block = lax.dynamic_index_in_dim(own, place, 0, keepdims=False)
    return block


def ring_near(block, first):
    from_minus = send_plane(block, 1)
    from_plus = send_plane(block, -1)
    far = send_plane(from_minus, 1) if first else send_plane(from_plus, -1)
    return [block, from_plus, far, from_minus]


def ring_far(block):
    return [block, send_plane(block, -1), send_plane(block, 2), send_plane(block, 1)]


def gather(own, place):
    block = gather_y(own, place)
    y_minus = send_y(block, 1)
    y_plus = send_y(block, -1)
    y_minus, y_plus = lax.optimization_barrier((y_minus, y_plus))
    y_far = send_y(after(block, y_minus, y_plus), 2)
    one = ring_near(y_plus, False)
    three = ring_near(y_minus, True)
    two = ring_far(y_far)
    return one + two + three, y_far


def block_of(own, blocks, dy, dq, quarter):
    if dy == 0:
        return own[lax.rem(quarter + dq, 4)]
    return blocks[(dy - 1) * 4 + dq][...]


def keys_kernel(where, tokens, own, *refs):
    blocks, (keys, values, memory) = refs[:12], refs[12:]
    y, quarter = where[0], where[1]
    for dq in range(4):
        total = None
        for dy in range(4):
            part = tokens[:, at(lax.rem(y + dy, 4), 512)]
            term = dot(part, block_of(own, blocks, dy, dq, quarter), 1, 0)
            total = term if total is None else total + term
        both = total.astype(BF)
        keys[:, dq * 256 : dq * 256 + 256] = both[:, :256]
        values[:, dq * 256 : dq * 256 + 256] = both[:, 256:]
        for head in range(2):
            low = head * HEAD
            memory[lax.rem(quarter + dq, 4) * 2 + head] = dot(
                both[:, low : low + HEAD], both[:, 256 + low : 256 + low + HEAD], 0, 0
            )


def queries_kernel(where, tokens, cotangent, own, *refs):
    blocks, (queries, grad_normed) = refs[:12], refs[12:]
    y, quarter = where[0], where[1]
    for dq in range(4):
        left = right = None
        for dy in range(4):
            cols = at(lax.rem(y + dy, 4), 512)
            block = block_of(own, blocks, dy, dq, quarter)
            one = dot(tokens[:, cols], block[:, :256], 1, 0)
            two = dot(cotangent[:, cols], block[:, 256:], 1, 0)
            left = one if left is None else left + one
            right = two if right is None else right + two
        queries[:, dq * 256 : dq * 256 + 256] = left.astype(BF)
        grad_normed[:, dq * 256 : dq * 256 + 256] = right


def attend_kernel(where, queries, grad_normed, memory, grad_queries, grad_memory):
    quarter = where[1]
    for head in range(8):
        cols = slice(head * HEAD, head * HEAD + HEAD)
        true_head = lax.rem(quarter * 2 + head, 8)
        query, mem, grad = queries[:, cols], memory[true_head], grad_normed[:, cols]
        attended = dot(query, mem, 1, 0)
        square = jnp.mean(attended * attended, axis=-1, keepdims=True)
        root_mean = jnp.sqrt(square + norm_eps)
        normed = attended / root_mean
        inner = jnp.mean(grad * normed, axis=-1, keepdims=True)
        grad_attended = ((grad - normed * inner) / root_mean).astype(BF)
        grad_memory[true_head] = dot(query, grad_attended, 0, 0)
        grad_queries[:, cols] = dot(grad_attended, mem, 1, 1).astype(BF)


def outer_kernel(where, tokens, values, product):
    quarter, core = where[1], where[2]
    for dq in range(4):
        cols = at(lax.rem(quarter + dq, 4), 256)
        for y in range(4):
            block = dot(tokens[:, y * 512 : y * 512 + 512], values[:, dq * 256 : dq * 256 + 256], 0, 0)
            block = block.astype(BF)
            for x in range(4):
                for z in range(4):
                    row = (x * 4 + z) * 32
                    spot = jnp.where(core == 0, x * 4 + z, z * 4 + x)
                    product[spot, y * 32 : y * 32 + 32, cols] = block[row : row + 32]


def query_grad_kernel(where, grad_queries, own, *refs):
    blocks, out = refs[:12], refs[12]
    y, quarter = where[0], where[1]
    for dy in range(4):
        total = None
        for dq in range(4):
            block = block_of(own, blocks, dy, dq, quarter)[:, :256]
            term = dot(grad_queries[:, dq * 256 : dq * 256 + 256], block, 1, 1)
            total = term if total is None else total + term
        true_y = lax.rem(y + dy, 4)
        out[true_y // 2, :, at(lax.rem(true_y, 2), 512)] = total


def input_grad_kernel(where, query_part, keys, values, grad_memory, own, *refs):
    blocks, out, both = refs[:12], refs[12], refs[13]
    y, quarter = where[0], where[1]
    for dq in range(4):
        for head in range(2):
            low = dq * 256 + head * HEAD
            mem = grad_memory[lax.rem(quarter + dq, 4) * 2 + head]
            grad_key = dot(values[:, low : low + HEAD], mem, 1, 1).astype(BF)
            grad_value = dot(keys[:, low : low + HEAD], mem, 1, 0).astype(BF)
            spot = head * HEAD
            both[dq, :, spot : spot + HEAD] = grad_key
            both[dq, :, 256 + spot : 256 + spot + HEAD] = grad_value
    for dy in range(4):
        true_y = lax.rem(y + dy, 4)
        cols = at(lax.rem(true_y, 2), 512)
        total = query_part[true_y // 2, :, cols]
        for dq in range(4):
            total = total + dot(both[dq], block_of(own, blocks, dy, dq, quarter), 1, 1)
        out[true_y // 2, :, cols] = total


def slice_grad_kernel(product, grad_memory, out):
    for head in range(8):
        cols = slice(head * HEAD, head * HEAD + HEAD)
        part = product[:, cols]
        high = part.astype(BF)
        low = (part - high.astype(F32)).astype(BF)
        mem = grad_memory[head]
        out[:, cols] = (dot(high, mem, 1, 1) + dot(low, mem, 1, 1)) * 0.25


def adam_kernel(where, master, moment, second, one, two, three, four, *outs):
    master_new, moment_new, second_new = outs
    core, x, z = where[2], where[3], where[4]
    for dx, blocks in enumerate((one, two, three, four)):
        for dz in range(4):
            first, other = dz, dx
            place_x = lax.rem(x + jnp.where(core == 0, first, other), 4)
            place_z = lax.rem(z + jnp.where(core == 0, other, first), 4)
            rows = at(place_x * 4 + place_z, 32)
            gradient = blocks[dz * 32 : dz * 32 + 32, :].astype(F32)
            held = master[rows, :]
            moved = beta_one * moment[rows, :] + (1.0 - beta_one) * gradient
            squared = beta_two * second[rows, :] + (1.0 - beta_two) * gradient * gradient
            update = moved / bias_one / (jnp.sqrt(squared / bias_two) + adam_eps)
            master_new[rows, :] = held - learn_rate * (update + weight_decay * held)
            moment_new[rows, :] = moved
            second_new[rows, :] = squared


def sum_over_context(partial):
    pieces = lax.all_to_all(partial.reshape(16, 64, HEAD), "context", 0, 0, tiled=True)
    mine = jnp.sum(pieces, axis=0).astype(BF)
    copies = jnp.broadcast_to(mine[None], (16, 64, HEAD))
    return lax.all_to_all(copies, "context", 0, 0, tiled=True).reshape(8, HEAD, HEAD)


def share_plane(block, cross):
    return [
        block,
        send_plane(block, -1, cross),
        send_plane(block, 2, cross),
        send_plane(block, 1, cross),
    ]


def local(
    tokens, cotangent, query_weight, key_master, value_weight, out_weight, key_moment, key_second
):
    tokens = tokens.reshape(512, 2048)
    cotangent = cotangent.reshape(512, 2048)
    y, context, core = (lax.axis_index(name) for name in ("dp", "context", "tensor"))
    x, z = context // 4, lax.rem(context, 4)
    quarter = jnp.where(core == 0, x, z)
    where = jnp.stack([y, quarter, core, x, z]).astype(jnp.int32)

    def quarters(left, right):
        parts = [w.reshape(512, 4, 256).transpose(1, 0, 2) for w in (left, right)]
        return jnp.concatenate(parts, axis=2)

    kv_own = quarters(key_master.astype(BF), value_weight)
    qo_own = quarters(query_weight, out_weight)

    kv_blocks, kv_sent = gather(kv_own, quarter)
    qo_blocks, _ = gather(after(qo_own, kv_sent), quarter)

    keys, values, partial = run(
        keys_kernel,
        [shape((512, 1024), BF), shape((512, 1024), BF), shape((8, HEAD, HEAD), F32)],
        [where, tokens, kv_own] + kv_blocks,
        4_400_000_000,
    )
    memory = sum_over_context(partial)
    queries, grad_normed = run(
        queries_kernel,
        [shape((512, 1024), BF), shape((512, 1024), F32)],
        [where, tokens, cotangent, qo_own] + qo_blocks,
        4_300_000_000,
    )
    grad_queries, partial = run(
        attend_kernel,
        [shape((512, 1024), BF), shape((8, HEAD, HEAD), F32)],
        [where, queries, grad_normed, memory],
        500_000_000,
    )
    grad_memory = sum_over_context(partial)

    product = run(
        outer_kernel, shape((16, 128, 1024), BF), [where, tokens, values], 2_150_000_000
    )
    pieces = lax.all_to_all(
        product.reshape(4, 512, 1024), CORE, 0, 0, tiled=True, axis_index_groups=plane_groups()
    )
    half = jnp.sum(pieces.astype(F32), axis=0).astype(BF)
    pieces = lax.all_to_all(
        half.reshape(4, 128, 1024), CORE, 0, 0, tiled=True, axis_index_groups=plane_groups(True)
    )
    product = jnp.sum(pieces.astype(F32), axis=0)

    query_part = run(
        query_grad_kernel,
        shape((2, 512, 1024), F32),
        [where, grad_queries, qo_own] + qo_blocks,
        2_150_000_000,
    )

    slice_grad = run(
        slice_grad_kernel, shape((128, 1024), F32), [product, grad_memory], 70_000_000, False
    )
    pieces = lax.all_to_all(slice_grad.reshape(4, 32, 1024), "dp", 0, 0, tiled=True)
    gradient = jnp.sum(pieces, axis=0).astype(BF)
    row = jnp.concatenate(share_plane(gradient, False), axis=0)
    whole = share_plane(row, True)

    input_terms = pl.pallas_call(
        input_grad_kernel,
        out_shape=shape((2, 512, 1024), F32),
        in_specs=[SMEM] + [VMEM] * 17,
        out_specs=VMEM,
        scratch_shapes=[pltpu.VMEM((4, 512, 512), BF)],
        compiler_params=pltpu.CompilerParams(vmem_limit_bytes=48 << 20),
        cost_estimate=pl.CostEstimate(
            flops=4_500_000_000, bytes_accessed=20 << 20, transcendentals=0
        ),
    )(where, query_part, keys, values, grad_memory, kv_own, *kv_blocks)
    sent = lax.dynamic_index_in_dim(input_terms, 1 - core, 0, keepdims=False)
    kept = lax.dynamic_index_in_dim(input_terms, core, 0, keepdims=False)
    arrived = lax.ppermute(sent, "tensor", [(0, 1), (1, 0)])
    input_grad = (kept + arrived).astype(BF).reshape(1, 512, 1024)

    state = shape((512, 1024), F32)
    master_new, moment_new, second_new = run(
        adam_kernel,
        [state, state, state],
        [where, key_master, key_moment, key_second] + whole,
        10_000_000,
    )
    return (input_grad, master_new, moment_new, second_new)


def solution(mesh):
    return jax.shard_map(
        local,
        mesh=mesh,
        in_specs=(
            P("dp", "context", None),
            P("dp", "context", None),
            P("dp", "tensor"),
            P("dp", "tensor"),
            P("dp", "tensor"),
            P("dp", "tensor"),
            P("dp", "tensor"),
            P("dp", "tensor"),
        ),
        out_specs=(
            P("dp", "context", "tensor"),
            P("dp", "tensor"),
            P("dp", "tensor"),
            P("dp", "tensor"),
        ),
        check_vma=False,
    )
```

time: 543 us -> 269 us (0.50)
  waiting for transfers between devices: 289 us -> 40.9 us
  blocking collectives: 150 us -> 56.3 us
  starting transfers between devices: 0.24 us -> 73 us
  Pallas kernels: 0 us -> 54.8 us
  matrix products: 44.5 us -> 0 us
  between operations: 14.3 us -> 1.22 us
    psum x2 -> x0, blocking collectives: 150 us -> none  [the longest x1 75.8 us: local(): grad_memory = lax.psum(local_grad_memory, 'context')]
    psum x1 -> x0, waiting for transfers between devices: 149 us -> none  [local(): whole_grad = lax.psum(product * scale_factor, ('dp', 'context'))]
    all_gather x4 -> x0, waiting for transfers between devices: 138 us -> none  [the longest x1 48.7 us: local(): lax.all_gather(key_master.astype(jnp.bfloat16), 'dp', axis=0, tiled=True)]
    all_to_all x0 -> x4, blocking collectives: none -> 56.3 us  [the longest x2 31.9 us: sum_over_context(): lax.all_to_all(partial.reshape(16, 64, HEAD), 'context', 0, 0, tiled=True)]
    pallas_call x0 -> x8, Pallas kernels: none -> 54.8 us  [the longest x7 44.2 us: run(): pl.pallas_call(kernel, out_shape=out_shape, in_specs=specs, out_specs=[VM...]
    ppermute x0 -> x31, starting transfers between devices: none -> 45.2 us  [the longest x24 35.6 us: send_plane(): return lax.ppermute(block, CORE, plane_pairs(shift, cross))]
    dot_general x14 -> x0, matrix products: 44.5 us -> none  [the longest x3 14.5 us: project(): product = jnp.dot(flat_tokens, weight, preferred_element_type=jnp.float32)]
    ppermute x0 -> x31, waiting for transfers between devices: none -> 36.6 us  [the longest x24 21.3 us: send_plane(): return lax.ppermute(block, CORE, plane_pairs(shift, cross))]
  transfers between devices with their start and end apart: 6 -> 34, of which waited for: 5 -> 15; matrix products, arithmetic and copies ran while one was open for 10% -> 8% of each run, Pallas kernels for 0% -> 17%
where the time goes in v1:
time: 269 us; the launch traced here: 265 us
  starting transfers between devices  73 us (27%)
  blocking collectives  56.3 us (21%)
  Pallas kernels  54.8 us (20%)
  waiting for transfers between devices  40.9 us (15%)
  local copies, waits for them, and re-layouts  24.5 us (9%)
  other arithmetic  14 us (5%)
    pallas_call x7, Pallas kernels, run(): pl.pallas_call(kernel, out_shape=out_shape, in_specs=specs, out_specs=[VM...  44.2 us
    ppermute x24, starting transfers between devices, send_plane(): return lax.ppermute(block, CORE, plane_pairs(shift, cross))  35.6 us
    all_to_all x2, blocking collectives, sum_over_context(): lax.all_to_all(partial.reshape(16, 64, HEAD), 'context', 0, 0, tiled=True)  31.9 us
    all_to_all x2, starting transfers between devices, sum_over_context(): lax.all_to_all(copies, 'context', 0, 0, tiled=True).reshape(8, HEAD, HEAD)  21.4 us
    ppermute x24, waiting for transfers between devices, send_plane(): return lax.ppermute(block, CORE, plane_pairs(shift, cross))  21.3 us
    ppermute x6, waiting for transfers between devices, send_y(): return lax.ppermute(block, 'dp', y_pairs(shift))  15.4 us
    unnamed x58, local copies, waits for them, and re-layouts  15.3 us
    all_to_all x1, blocking collectives, local(): lax.all_to_all(half.reshape(4, 128, 1024), CORE, 0, 0, tiled=True, axis_i...  13.9 us
  transfers between devices with their start and end apart: 34, of which 15 were waited for; matrix products, arithmetic and copies ran while one was open for 8% of the time, Pallas kernels for 17%

profile of v1, /device:TPU:2, one launch (start us, length us, event | category | flops | bytes accessed | tf_op | source)
XLA Modules:
  0.0 264.7 jit_solution(13280701714882053165)
XLA Ops:
  0.7 1.8 copy.24
  3.0 1.9 copy.26
  6.4 1.6 collective-permute-start
  7.9 1.7 collective-permute-start.1
  9.6 11.9 %collective-permute-done.refs_8_ = bf16[512,512]{1,0:T(8,128)(2,1)S(1)} collective-permute-done((bf16[512,512]{1,0:T(8,128)(2,1)}, bf16[512,512]{1,0:T(8,128)(2,1)S(1)}, u32[]{:S(2)}, u32[]{:S(2)}) %collective-permute-start) | collective-permute-done | bytes 524320 | tf_op jit(solution)/shard_map/ppermute | solution.py:59
  21.5 2.9 %collective-permute-start.2 = (bf16[512,512]{1,0:T(8,128)(2,1)}, bf16[512,512]{1,0:T(8,128)(2,1)S(1)}, u32[]{:S(2)}, u32[]{:S(2)}) collective-permute-start(bf16[512,512]{1,0:T(8,128)(2,1)} %fusion.3), channel_id=1, source_target_pairs={{0,64},{32,96},{64,0},{96,32},{1,65},{33,97},{65,1},{97,33},{2,66}... | collective-permute-start | bytes 1572872 | tf_op jit(solution)/shard_map/ppermute | solution.py:59
  30.6 1.7 pad_maximum_fusion.1.own
  32.3 1.6 collective-permute-start.17
  38.1 2.0 collective-permute-start.4
  40.2 2.1 collective-permute-done.17.refs_3_
  42.3 3.2 %collective-permute-start.16 = (bf16[512,512]{1,0:T(8,128)(2,1)S(1)}, bf16[512,512]{1,0:T(8,128)(2,1)S(1)}, u32[]{:S(2)}, u32[]{:S(2)}) collective-permute-start(bf16[512,512]{1,0:T(8,128)(2,1)S(1)} %collective-permute-done.15.refs_1_), channel_id=1, source_target_pairs={{0,24},{1,7},{2,26},{3,1},{4,28},{5,3},{6,30},{7,5},{8,0},{9,15},{... | collective-permute-start | bytes 1572872 | tf_op jit(solution)/shard_map/ppermute | solution.py:63
  45.7 2.2 collective-permute-done.22.refs_11_
  47.9 1.7 collective-permute-start.19
  49.6 3.2 %collective-permute-done.3.refs_8_ = bf16[512,512]{1,0:T(8,128)(2,1)} collective-permute-done((bf16[512,512]{1,0:T(8,128)(2,1)}, bf16[512,512]{1,0:T(8,128)(2,1)}, u32[]{:S(2)}, u32[]{:S(2)}) %collective-permute-start.3) | collective-permute-done | bytes 524320 | tf_op jit(solution)/shard_map/ppermute | solution.py:59
  58.6 2.5 collective-permute-start.5
  61.1 2.3 collective-permute-done.19.refs_6_
  65.0 3.2 %collective-permute-start.12 = (bf16[512,512]{1,0:T(8,128)(2,1)}, bf16[512,512]{1,0:T(8,128)(2,1)}, u32[]{:S(2)}, u32[]{:S(2)}) collective-permute-start(bf16[512,512]{1,0:T(8,128)(2,1)} %collective-permute-done.3.refs_8_), channel_id=1, source_target_pairs={{0,24},{1,7},{2,26},{3,1},{4,28},{5,3},{6,30},{7,5},{8,0},{9,15},{... | collective-permute-start | bytes 1572872 | tf_op jit(solution)/shard_map/ppermute | solution.py:63
  71.2 3.2 %pad_maximum_fusion.own = bf16[4,512,512]{2,1,0:T(8,128)(2,1)} fusion(bf16[4,512,256]{2,1,0:T(8,128)(2,1)} %bitcast.48, bf16[4,512,256]{2,1,0:T(8,128)(2,1)} %bitcast.46), kind=kLoop, calls=%fused_computation.1 | loop fusion | flops 4194304 | bytes 4194304 | tf_op jit(solution)/shard_map/concatenate | solution.py:289
  74.3 2.1 collective-permute-start.9
  76.4 2.1 collective-permute-start.10
  78.6 2.5 collective-permute-start.11
  81.1 2.3 collective-permute-start.14
  83.4 9.1 %shard_map.112 = (bf16[512,1024]{1,0:T(8,128)(2,1)}, bf16[512,1024]{1,0:T(8,128)(2,1)}, f32[8,128,128]{2,1,0:T(8,128)S(1)}) custom-call(s32[5]{0:T(128)S(1)} %stack.23.where, bf16[512,2048]{1,0:T(8,128)(2,1)} %bitcast.42, bf16[4,512,512]{2,1,0:T(8,128)(2,1)} %pad_maximum_fusion.own, bf16[512,512]{1,0:T(8,128)(2,1)S(1)} %collective-permute-done.1.refs_0_, ...), custom_call_target="tpu_custom_call" | custom-call | flops 4400000000 | bytes 13107220 | tf_op jit(solution)/shard_map/pallas_call | solution.py:75
  92.5 16.9 %all_to_all.35 = f32[16,64,128]{2,1,0:T(8,128)S(1)} all-to-all(f32[16,64,128]{2,1,0:T(8,128)S(1)} %bitcast.41), channel_id=1, replica_groups=mesh['dp'=4,'context'=16,'tensor'=2] {'context'}, dimensions={0} | all-to-all | bytes 1048576 | tf_op jit(solution)/shard_map/all_to_all | solution.py:262
  110.2 5.7 %all-to-all-start.1 = ((bf16[16,64,128]{2,1,0:T(8,128)(2,1)}), bf16[16,64,128]{2,1,0:T(8,128)(2,1)S(1)}, u32[]{:S(2)}, u32[]{:S(2)}) async-start(bf16[16,64,128]{2,1,0:T(8,128)(2,1)} %broadcast_in_dim.4), calls=%async_computation.1 | async-start | bytes 524288 | tf_op jit(solution)/shard_map/all_to_all | solution.py:265
  115.9 10.7 %shard_map.111 = (bf16[512,1024]{1,0:T(8,128)(2,1)}, f32[512,1024]{1,0:T(8,128)}) custom-call(s32[5]{0:T(128)S(1)} %stack.23.where, bf16[512,2048]{1,0:T(8,128)(2,1)} %bitcast.43, bf16[512,2048]{1,0:T(8,128)(2,1)} %bitcast.57, bf16[4,512,512]{2,1,0:T(8,128)(2,1)} %copy-done.23, bf16[512,512]{1,0:T(8,128)(2,1)} %collective-permute-done.4.refs_0_, ...), custom_call_target="tpu_custom_call" | custom-call | flops 4300000256 | bytes 15728660 | tf_op jit(solution)/shard_map/pallas_call | solution.py:75
  126.6 1.6 copy-done.1
  129.4 4.4 %shard_map.113 = (bf16[512,1024]{1,0:T(8,128)(2,1)S(1)}, f32[8,128,128]{2,1,0:T(8,128)S(1)}) custom-call(s32[5]{0:T(128)S(1)} %stack.23.where, bf16[512,1024]{1,0:T(8,128)(2,1)S(1)} %copy-done.4, f32[512,1024]{1,0:T(8,128)S(1)} %copy-done.1, bf16[8,128,128]{2,1,0:T(8,128)(2,1)S(1)} %bitcast.39), custom_call_target="tpu_custom_call" | custom-call | flops 500000000 | bytes 4980756 | tf_op jit(solution)/shard_map/pallas_call | solution.py:75
  134.8 15.0 %all_to_all.36 = f32[16,64,128]{2,1,0:T(8,128)} all-to-all(f32[16,64,128]{2,1,0:T(8,128)S(1)} %bitcast.40), channel_id=1, replica_groups=mesh['dp'=4,'context'=16,'tensor'=2] {'context'}, dimensions={0} | all-to-all | bytes 1048576 | tf_op jit(solution)/shard_map/all_to_all | solution.py:262
  151.6 15.7 %all-to-all-start.3 = ((bf16[16,64,128]{2,1,0:T(8,128)(2,1)}), bf16[16,64,128]{2,1,0:T(8,128)(2,1)S(1)}, u32[]{:S(2)}, u32[]{:S(2)}) async-start(bf16[16,64,128]{2,1,0:T(8,128)(2,1)} %broadcast_in_dim.5), calls=%async_computation.3 | async-start | bytes 524288 | tf_op jit(solution)/shard_map/all_to_all | solution.py:265
  167.4 1.6 copy-done.22
  169.0 5.3 %shard_map.116 = bf16[16,128,1024]{2,1,0:T(8,128)(2,1)} custom-call(s32[5]{0:T(128)S(1)} %stack.23.where, bf16[512,2048]{1,0:T(8,128)(2,1)S(1)} %bitcast.44, bf16[512,1024]{1,0:T(8,128)(2,1)S(1)} %copy-done.3), custom_call_target="tpu_custom_call" | custom-call | flops 2150000128 | bytes 7340052 | tf_op jit(solution)/shard_map/pallas_call | solution.py:75
  174.3 6.4 %all-to-all-start.4 = ((bf16[4,512,1024]{2,1,0:T(8,128)(2,1)}), bf16[4,512,1024]{2,1,0:T(8,128)(2,1)}, u32[]{:S(2)}, u32[]{:S(2)}) async-start(bf16[4,512,1024]{2,1,0:T(8,128)(2,1)} %bitcast.50), calls=%async_computation.4 | async-start | bytes 8388608 | tf_op jit(solution)/shard_map/all_to_all | solution.py:321
  180.8 8.3 %shard_map.114.query_part = f32[2,512,1024]{2,1,0:T(8,128)} custom-call(s32[5]{0:T(128)S(1)} %stack.23.where, bf16[512,1024]{1,0:T(8,128)(2,1)} %copy-done.5, bf16[4,512,512]{2,1,0:T(8,128)(2,1)} %copy-done.23, bf16[512,512]{1,0:T(8,128)(2,1)} %collective-permute-done.4.refs_0_, bf16[512,512]{1,0:T(8,128)(2,1)} %collective-permute-done.5.refs_1_, ...), custom_call_target="tpu_custom_call" | custom-call | flops 2150000128 | bytes 13631508 | tf_op jit(solution)/shard_map/pallas_call | solution.py:75
  189.1 10.6 %shard_map.115 = f32[2,512,1024]{2,1,0:T(8,128)} custom-call(s32[5]{0:T(128)S(1)} %stack.23.where, f32[2,512,1024]{2,1,0:T(8,128)} %shard_map.114.query_part, bf16[512,1024]{1,0:T(8,128)(2,1)} %get-tuple-element.32.keys, bf16[512,1024]{1,0:T(8,128)(2,1)} %get-tuple-element.33.values, bf16[8,128,128]{2,1,0:T(8,128)(2,1)S(1)} %bitcast.36, ...), custom_call_target="tpu_custom_call" | custom-call | flops 4499999744 | bytes 20971520 | tf_op jit(solution)/shard_map/pallas_call | solution.py:345
  199.7 3.2 %dynamic-slice_bitcast_fusion = f32[512,1024]{1,0:T(8,128)} fusion(f32[2,512,1024]{2,1,0:T(8,128)} %shard_map.115, s32[]{:T(128)S(6)} %select_n.24), kind=kLoop, calls=%fused_computation.7 | loop fusion | bytes 4194308 | tf_op jit(solution)/shard_map/jit(dynamic_index_in_dim)/squeeze | solution.py:356
  202.9 4.2 %all-to-all-done.4 = bf16[4,512,1024]{2,1,0:T(8,128)(2,1)} async-done(((bf16[4,512,1024]{2,1,0:T(8,128)(2,1)}), bf16[4,512,1024]{2,1,0:T(8,128)(2,1)}, u32[]{:S(2)}, u32[]{:S(2)}) %all-to-all-start.4) | async-done | bytes 4194336 | tf_op jit(solution)/shard_map/all_to_all | solution.py:321
  207.1 3.3 %reduce_sum.50 = bf16[512,1024]{1,0:T(8,128)(2,1)S(1)} reduce(bf16[4,512,1024]{2,1,0:T(8,128)(2,1)} %all-to-all-done.4, bf16[]{:T(256)} %constant.49.clone.1), dimensions={0}, to_apply=%region_2.3 | reduce | flops 1572864 | bytes 5242882 | tf_op jit(solution)/shard_map/reduce_sum | solution.py:324
  210.4 13.9 %all_to_all.37 = bf16[4,128,1024]{2,1,0:T(8,128)(2,1)S(1)} all-to-all(bf16[4,128,1024]{2,1,0:T(8,128)(2,1)S(1)} %bitcast.56), channel_id=1, replica_groups={{0,2,4,6},{1,9,17,25},{8,10,12,14},{3,11,19,27},{16,18,20,22},{5,13,21,..., dimensions={0} | all-to-all | bytes 2097152 | tf_op jit(solution)/shard_map/all_to_all | solution.py:325
  225.0 10.5 %all_to_all.38 = f32[4,32,1024]{2,1,0:T(8,128)S(1)} all-to-all(f32[4,32,1024]{2,1,0:T(8,128)S(1)} %bitcast.38), channel_id=1, replica_groups=mesh['dp'=4,'context'=16,'tensor'=2] {'dp'}, dimensions={0} | all-to-all | bytes 1048576 | tf_op jit(solution)/shard_map/all_to_all | solution.py:340
  235.6 3.5 %collective-permute-start.26 = (bf16[32,1024]{1,0:T(8,128)(2,1)S(1)}, bf16[32,1024]{1,0:T(8,128)(2,1)S(1)}, u32[]{:S(2)}, u32[]{:S(2)}) collective-permute-start(bf16[32,1024]{1,0:T(8,128)(2,1)S(1)} %reduce_sum.52), channel_id=1, source_target_pairs={{0,16},{1,5},{2,18},{3,7},{4,20},{5,1},{6,22},{7,3},{8,24},{9,13},... | collective-permute-start | bytes 196616 | tf_op jit(solution)/shard_map/ppermute | solution.py:63
  239.9 2.3 collective-permute-done.26
  242.2 3.2 %collective-permute-done.25 = bf16[32,1024]{1,0:T(8,128)(2,1)S(1)} collective-permute-done((bf16[32,1024]{1,0:T(8,128)(2,1)S(1)}, bf16[32,1024]{1,0:T(8,128)(2,1)S(1)}, u32[]{:S(2)}, u32[]{:S(2)}) %collective-permute-start.25) | collective-permute-done | bytes 65568 | tf_op jit(solution)/shard_map/ppermute | solution.py:63
  245.4 2.5 collective-permute-start.28
  248.9 3.5 %fusion.1 = bf16[1,512,1024]{2,1,0:T(8,128)(2,1)} fusion(f32[512,1024]{1,0:T(8,128)} %collective-permute-done.24, f32[2,512,1024]{2,1,0:T(8,128)} %shard_map.115, s32[]{:T(128)S(6)} %select_n.23), kind=kLoop, calls=%fused_computation.8 | loop fusion | flops 1048576 | bytes 5242884 | tf_op jit(solution)/shard_map/reshape | solution.py:359
  252.4 2.3 collective-permute-done.28.two
  255.9 2.7 %collective-permute-done.30.four = bf16[128,1024]{1,0:T(8,128)(2,1)S(1)} collective-permute-done((bf16[128,1024]{1,0:T(8,128)(2,1)S(1)}, bf16[128,1024]{1,0:T(8,128)(2,1)S(1)}, u32[]{:S(2)}, u32[]{:S(2)}) %collective-permute-start.30) | collective-permute-done | bytes 262176 | tf_op jit(solution)/shard_map/ppermute | solution.py:63
  258.6 5.9 %shard_map.118 = (f32[512,1024]{1,0:T(8,128)}, f32[512,1024]{1,0:T(8,128)}, f32[512,1024]{1,0:T(8,128)}) custom-call(s32[5]{0:T(128)S(1)} %stack.23.where, f32[512,1024]{1,0:T(8,128)S(1)} %copy-done, f32[512,1024]{1,0:T(8,128)S(1)} %copy-done.2, f32[512,1024]{1,0:T(8,128)} %second.1, bf16[128,1024]{1,0:T(8,128)(2,1)S(1)} %pad_maximum_fusion.2.one, ...), custom_call_target="tpu_custom_call" | custom-call | flops 10000000 | bytes 13631508 | tf_op jit(solution)/shard_map/pallas_call | solution.py:75
  (109 shorter events, 31.6 us)
Async XLA Ops:
  5.4 16.1 %copy-start.25 = (bf16[512,4,256]{2,0,1:T(8,128)(2,1)}, bf16[512,4,256]{2,0,1:T(8,128)(2,1)S(1)}, u32[]{:S(2)}) copy-start(bf16[512,4,256]{2,0,1:T(8,128)(2,1)S(1)} %copy.27) | copy-start | bytes 3145732
  6.4 15.1 %collective-permute-start = (bf16[512,512]{1,0:T(8,128)(2,1)}, bf16[512,512]{1,0:T(8,128)(2,1)S(1)}, u32[]{:S(2)}, u32[]{:S(2)}) collective-permute-start(bf16[512,512]{1,0:T(8,128)(2,1)} %fusion.3), channel_id=1, source_target_pairs={{0,32},{32,64},{64,96},{96,0},{1,33},{33,65},{65,97},{97,1},{2,34}... | collective-permute-start | bytes 1572872 | tf_op jit(solution)/shard_map/ppermute | solution.py:59
  7.9 13.6 %collective-permute-start.1 = (bf16[512,512]{1,0:T(8,128)(2,1)}, bf16[512,512]{1,0:T(8,128)(2,1)S(1)}, u32[]{:S(2)}, u32[]{:S(2)}) collective-permute-start(bf16[512,512]{1,0:T(8,128)(2,1)} %fusion.3), channel_id=1, source_target_pairs={{0,96},{32,0},{64,32},{96,64},{1,97},{33,1},{65,33},{97,65},{2,98}... | collective-permute-start | bytes 1572872 | tf_op jit(solution)/shard_map/ppermute | solution.py:59
  21.5 14.6 %collective-permute-start.2 = (bf16[512,512]{1,0:T(8,128)(2,1)}, bf16[512,512]{1,0:T(8,128)(2,1)S(1)}, u32[]{:S(2)}, u32[]{:S(2)}) collective-permute-start(bf16[512,512]{1,0:T(8,128)(2,1)} %fusion.3), channel_id=1, source_target_pairs={{0,64},{32,96},{64,0},{96,32},{1,65},{33,97},{65,1},{97,33},{2,66}... | collective-permute-start | bytes 1572872 | tf_op jit(solution)/shard_map/ppermute | solution.py:59
  24.4 13.7 %collective-permute-start.15 = (bf16[512,512]{1,0:T(8,128)(2,1)S(1)}, bf16[512,512]{1,0:T(8,128)(2,1)S(1)}, u32[]{:S(2)}, u32[]{:S(2)}) collective-permute-start(bf16[512,512]{1,0:T(8,128)(2,1)S(1)} %collective-permute-done.1.refs_0_), channel_id=1, source_target_pairs={{0,24},{1,7},{2,26},{3,1},{4,28},{5,3},{6,30},{7,5},{8,0},{9,15},{... | collective-permute-start | bytes 1572872 | tf_op jit(solution)/shard_map/ppermute | solution.py:63
  32.3 32.0 %copy-start.23 = (bf16[4,512,512]{2,1,0:T(8,128)(2,1)}, bf16[4,512,512]{2,1,0:T(8,128)(2,1)S(1)}, u32[]{:S(2)}) copy-start(bf16[4,512,512]{2,1,0:T(8,128)(2,1)S(1)} %pad_maximum_fusion.1.own) | copy-start | bytes 6291460
  32.3 10.0 %collective-permute-start.17 = (bf16[512,512]{1,0:T(8,128)(2,1)S(1)}, bf16[512,512]{1,0:T(8,128)(2,1)S(1)}, u32[]{:S(2)}, u32[]{:S(2)}) collective-permute-start(bf16[512,512]{1,0:T(8,128)(2,1)S(1)} %collective-permute-done.1.refs_0_), channel_id=1, source_target_pairs={{0,8},{1,3},{2,10},{3,5},{4,12},{5,7},{6,14},{7,1},{8,16},{9,11},{... | collective-permute-start | bytes 1572872 | tf_op jit(solution)/shard_map/ppermute | solution.py:63
  33.8 11.7 %collective-permute-start.21 = (bf16[512,512]{1,0:T(8,128)(2,1)S(1)}, bf16[512,512]{1,0:T(8,128)(2,1)S(1)}, u32[]{:S(2)}, u32[]{:S(2)}) collective-permute-start(bf16[512,512]{1,0:T(8,128)(2,1)S(1)} %collective-permute-done.refs_8_), channel_id=1, source_target_pairs={{0,24},{1,7},{2,26},{3,1},{4,28},{5,3},{6,30},{7,5},{8,0},{9,15},{... | collective-permute-start | bytes 1572872 | tf_op jit(solution)/shard_map/ppermute | solution.py:63
  35.2 12.7 %collective-permute-start.22 = (bf16[512,512]{1,0:T(8,128)(2,1)S(1)}, bf16[512,512]{1,0:T(8,128)(2,1)S(1)}, u32[]{:S(2)}, u32[]{:S(2)}) collective-permute-start(bf16[512,512]{1,0:T(8,128)(2,1)S(1)} %collective-permute-done.refs_8_), channel_id=1, source_target_pairs={{0,8},{1,3},{2,10},{3,5},{4,12},{5,7},{6,14},{7,1},{8,16},{9,11},{... | collective-permute-start | bytes 1572872 | tf_op jit(solution)/shard_map/ppermute | solution.py:63
  36.9 15.9 %collective-permute-start.3 = (bf16[512,512]{1,0:T(8,128)(2,1)}, bf16[512,512]{1,0:T(8,128)(2,1)}, u32[]{:S(2)}, u32[]{:S(2)}) collective-permute-start(bf16[512,512]{1,0:T(8,128)(2,1)} %dynamic-slice_bitcast_fusion.1), channel_id=1, source_target_pairs={{0,32},{32,64},{64,96},{96,0},{1,33},{33,65},{65,97},{97,1},{2,34}... | collective-permute-start | bytes 1572872 | tf_op jit(solution)/shard_map/ppermute | solution.py:59
  38.1 16.2 %collective-permute-start.4 = (bf16[512,512]{1,0:T(8,128)(2,1)}, bf16[512,512]{1,0:T(8,128)(2,1)}, u32[]{:S(2)}, u32[]{:S(2)}) collective-permute-start(bf16[512,512]{1,0:T(8,128)(2,1)} %dynamic-slice_bitcast_fusion.1), channel_id=1, source_target_pairs={{0,96},{32,0},{64,32},{96,64},{1,97},{33,1},{65,33},{97,65},{2,98}... | collective-permute-start | bytes 1572872 | tf_op jit(solution)/shard_map/ppermute | solution.py:59
  42.3 41.1 %copy-start.6 = (bf16[512,512]{1,0:T(8,128)(2,1)}, bf16[512,512]{1,0:T(8,128)(2,1)S(1)}, u32[]{:S(2)}) copy-start(bf16[512,512]{1,0:T(8,128)(2,1)S(1)} %collective-permute-done.17.refs_3_) | copy-start | bytes 1572868
  42.3 13.2 %collective-permute-start.16 = (bf16[512,512]{1,0:T(8,128)(2,1)S(1)}, bf16[512,512]{1,0:T(8,128)(2,1)S(1)}, u32[]{:S(2)}, u32[]{:S(2)}) collective-permute-start(bf16[512,512]{1,0:T(8,128)(2,1)S(1)} %collective-permute-done.15.refs_1_), channel_id=1, source_target_pairs={{0,24},{1,7},{2,26},{3,1},{4,28},{5,3},{6,30},{7,5},{8,0},{9,15},{... | collective-permute-start | bytes 1572872 | tf_op jit(solution)/shard_map/ppermute | solution.py:63
  45.5 37.9 %copy-start.8 = (bf16[512,512]{1,0:T(8,128)(2,1)}, bf16[512,512]{1,0:T(8,128)(2,1)S(1)}, u32[]{:S(2)}) copy-start(bf16[512,512]{1,0:T(8,128)(2,1)S(1)} %collective-permute-done.21.refs_9_) | copy-start | bytes 1572868
  45.5 12.3 %collective-permute-start.18 = (bf16[512,512]{1,0:T(8,128)(2,1)S(1)}, bf16[512,512]{1,0:T(8,128)(2,1)S(1)}, u32[]{:S(2)}, u32[]{:S(2)}) collective-permute-start(bf16[512,512]{1,0:T(8,128)(2,1)S(1)} %collective-permute-done.2.refs_4_), channel_id=1, source_target_pairs={{0,24},{1,7},{2,26},{3,1},{4,28},{5,3},{6,30},{7,5},{8,0},{9,15},{... | collective-permute-start | bytes 1572872 | tf_op jit(solution)/shard_map/ppermute | solution.py:63
  47.9 20.3 %copy-start.26 = (bf16[512,512]{1,0:T(8,128)(2,1)}, bf16[512,512]{1,0:T(8,128)(2,1)S(1)}, u32[]{:S(2)}) copy-start(bf16[512,512]{1,0:T(8,128)(2,1)S(1)} %collective-permute-done.22.refs_11_) | copy-start | bytes 1572868
  47.9 15.5 %collective-permute-start.19 = (bf16[512,512]{1,0:T(8,128)(2,1)S(1)}, bf16[512,512]{1,0:T(8,128)(2,1)S(1)}, u32[]{:S(2)}, u32[]{:S(2)}) collective-permute-start(bf16[512,512]{1,0:T(8,128)(2,1)S(1)} %collective-permute-done.2.refs_4_), channel_id=1, source_target_pairs={{0,16},{1,5},{2,18},{3,7},{4,20},{5,1},{6,22},{7,3},{8,24},{9,13},... | collective-permute-start | bytes 1572872 | tf_op jit(solution)/shard_map/ppermute | solution.py:63
  52.8 11.4 %collective-permute-start.20 = (bf16[512,512]{1,0:T(8,128)(2,1)S(1)}, bf16[512,512]{1,0:T(8,128)(2,1)S(1)}, u32[]{:S(2)}, u32[]{:S(2)}) collective-permute-start(bf16[512,512]{1,0:T(8,128)(2,1)S(1)} %collective-permute-done.2.refs_4_), channel_id=1, source_target_pairs={{0,8},{1,3},{2,10},{3,5},{4,12},{5,7},{6,14},{7,1},{8,16},{9,11},{... | collective-permute-start | bytes 1572872 | tf_op jit(solution)/shard_map/ppermute | solution.py:63
  54.3 15.4 %collective-permute-start.23 = (bf16[512,512]{1,0:T(8,128)(2,1)S(1)}, bf16[512,512]{1,0:T(8,128)(2,1)}, u32[]{:S(2)}, u32[]{:S(2)}) collective-permute-start(bf16[512,512]{1,0:T(8,128)(2,1)S(1)} %collective-permute-done.22.refs_11_), channel_id=1, source_target_pairs={{0,8},{1,3},{2,10},{3,5},{4,12},{5,7},{6,14},{7,1},{8,16},{9,11},{... | collective-permute-start | bytes 1572872 | tf_op jit(solution)/shard_map/ppermute | solution.py:63
  56.3 18.0 %collective-permute-start.8 = (bf16[512,512]{1,0:T(8,128)(2,1)}, bf16[512,512]{1,0:T(8,128)(2,1)}, u32[]{:S(2)}, u32[]{:S(2)}) collective-permute-start(bf16[512,512]{1,0:T(8,128)(2,1)} %dynamic-slice_bitcast_fusion.1), channel_id=1, source_target_pairs={{0,64},{32,96},{64,0},{96,32},{1,65},{33,97},{65,1},{97,33},{2,66}... | collective-permute-start | bytes 1572872 | tf_op jit(solution)/shard_map/ppermute | solution.py:59
  58.6 17.8 %collective-permute-start.5 = (bf16[512,512]{1,0:T(8,128)(2,1)}, bf16[512,512]{1,0:T(8,128)(2,1)}, u32[]{:S(2)}, u32[]{:S(2)}) collective-permute-start(bf16[512,512]{1,0:T(8,128)(2,1)} %collective-permute-done.4.refs_0_), channel_id=1, source_target_pairs={{0,24},{1,7},{2,26},{3,1},{4,28},{5,3},{6,30},{7,5},{8,0},{9,15},{... | collective-permute-start | bytes 1572872 | tf_op jit(solution)/shard_map/ppermute | solution.py:63
  64.2 14.3 %collective-permute-start.7 = (bf16[512,512]{1,0:T(8,128)(2,1)}, bf16[512,512]{1,0:T(8,128)(2,1)}, u32[]{:S(2)}, u32[]{:S(2)}) collective-permute-start(bf16[512,512]{1,0:T(8,128)(2,1)} %collective-permute-done.4.refs_0_), channel_id=1, source_target_pairs={{0,8},{1,3},{2,10},{3,5},{4,12},{5,7},{6,14},{7,1},{8,16},{9,11},{... | collective-permute-start | bytes 1572872 | tf_op jit(solution)/shard_map/ppermute | solution.py:63
  65.0 16.1 %collective-permute-start.12 = (bf16[512,512]{1,0:T(8,128)(2,1)}, bf16[512,512]{1,0:T(8,128)(2,1)}, u32[]{:S(2)}, u32[]{:S(2)}) collective-permute-start(bf16[512,512]{1,0:T(8,128)(2,1)} %collective-permute-done.3.refs_8_), channel_id=1, source_target_pairs={{0,24},{1,7},{2,26},{3,1},{4,28},{5,3},{6,30},{7,5},{8,0},{9,15},{... | collective-permute-start | bytes 1572872 | tf_op jit(solution)/shard_map/ppermute | solution.py:63
  69.7 11.5 %collective-permute-start.13 = (bf16[512,512]{1,0:T(8,128)(2,1)}, bf16[512,512]{1,0:T(8,128)(2,1)}, u32[]{:S(2)}, u32[]{:S(2)}) collective-permute-start(bf16[512,512]{1,0:T(8,128)(2,1)} %collective-permute-done.3.refs_8_), channel_id=1, source_target_pairs={{0,8},{1,3},{2,10},{3,5},{4,12},{5,7},{6,14},{7,1},{8,16},{9,11},{... | collective-permute-start | bytes 1572872 | tf_op jit(solution)/shard_map/ppermute | solution.py:63
  71.2 12.2 %copy-start.11 = (bf16[512,512]{1,0:T(8,128)(2,1)S(1)}, bf16[512,512]{1,0:T(8,128)(2,1)}, u32[]{:S(2)}) copy-start(bf16[512,512]{1,0:T(8,128)(2,1)} %copy-done.10) | copy-start | bytes 1572868
  71.2 12.2 %copy-start.14 = (bf16[512,512]{1,0:T(8,128)(2,1)S(1)}, bf16[512,512]{1,0:T(8,128)(2,1)}, u32[]{:S(2)}) copy-start(bf16[512,512]{1,0:T(8,128)(2,1)} %copy-done.13) | copy-start | bytes 1572868
  71.2 12.2 %copy-start.17 = (bf16[512,512]{1,0:T(8,128)(2,1)S(1)}, bf16[512,512]{1,0:T(8,128)(2,1)}, u32[]{:S(2)}) copy-start(bf16[512,512]{1,0:T(8,128)(2,1)} %copy-done.16) | copy-start | bytes 1572868
  71.2 12.2 %copy-start.20 = (bf16[512,512]{1,0:T(8,128)(2,1)S(1)}, bf16[512,512]{1,0:T(8,128)(2,1)}, u32[]{:S(2)}) copy-start(bf16[512,512]{1,0:T(8,128)(2,1)} %copy-done.19) | copy-start | bytes 1572868
  74.3 41.5 %collective-permute-start.9 = (bf16[512,512]{1,0:T(8,128)(2,1)}, bf16[512,512]{1,0:T(8,128)(2,1)}, u32[]{:S(2)}, u32[]{:S(2)}) collective-permute-start(bf16[512,512]{1,0:T(8,128)(2,1)} %collective-permute-done.8.refs_4_), channel_id=1, source_target_pairs={{0,24},{1,7},{2,26},{3,1},{4,28},{5,3},{6,30},{7,5},{8,0},{9,15},{... | collective-permute-start | bytes 1572872 | tf_op jit(solution)/shard_map/ppermute | solution.py:63
  76.4 39.4 %collective-permute-start.10 = (bf16[512,512]{1,0:T(8,128)(2,1)}, bf16[512,512]{1,0:T(8,128)(2,1)}, u32[]{:S(2)}, u32[]{:S(2)}) collective-permute-start(bf16[512,512]{1,0:T(8,128)(2,1)} %collective-permute-done.8.refs_4_), channel_id=1, source_target_pairs={{0,16},{1,5},{2,18},{3,7},{4,20},{5,1},{6,22},{7,3},{8,24},{9,13},... | collective-permute-start | bytes 1572872 | tf_op jit(solution)/shard_map/ppermute | solution.py:63
  78.6 37.3 %collective-permute-start.11 = (bf16[512,512]{1,0:T(8,128)(2,1)}, bf16[512,512]{1,0:T(8,128)(2,1)}, u32[]{:S(2)}, u32[]{:S(2)}) collective-permute-start(bf16[512,512]{1,0:T(8,128)(2,1)} %collective-permute-done.8.refs_4_), channel_id=1, source_target_pairs={{0,8},{1,3},{2,10},{3,5},{4,12},{5,7},{6,14},{7,1},{8,16},{9,11},{... | collective-permute-start | bytes 1572872 | tf_op jit(solution)/shard_map/ppermute | solution.py:63
  81.1 34.7 %collective-permute-start.6 = (bf16[512,512]{1,0:T(8,128)(2,1)}, bf16[512,512]{1,0:T(8,128)(2,1)}, u32[]{:S(2)}, u32[]{:S(2)}) collective-permute-start(bf16[512,512]{1,0:T(8,128)(2,1)} %collective-permute-done.5.refs_1_), channel_id=1, source_target_pairs={{0,24},{1,7},{2,26},{3,1},{4,28},{5,3},{6,30},{7,5},{8,0},{9,15},{... | collective-permute-start | bytes 1572872 | tf_op jit(solution)/shard_map/ppermute | solution.py:63
  81.1 34.7 %collective-permute-start.14 = (bf16[512,512]{1,0:T(8,128)(2,1)}, bf16[512,512]{1,0:T(8,128)(2,1)}, u32[]{:S(2)}, u32[]{:S(2)}) collective-permute-start(bf16[512,512]{1,0:T(8,128)(2,1)} %collective-permute-done.13.refs_11_), channel_id=1, source_target_pairs={{0,8},{1,3},{2,10},{3,5},{4,12},{5,7},{6,14},{7,1},{8,16},{9,11},{... | collective-permute-start | bytes 1572872 | tf_op jit(solution)/shard_map/ppermute | solution.py:63
  110.2 16.4 %all-to-all-start.1 = ((bf16[16,64,128]{2,1,0:T(8,128)(2,1)}), bf16[16,64,128]{2,1,0:T(8,128)(2,1)S(1)}, u32[]{:S(2)}, u32[]{:S(2)}) async-start(bf16[16,64,128]{2,1,0:T(8,128)(2,1)} %broadcast_in_dim.4), calls=%async_computation.1 | async-start | bytes 524288 | tf_op jit(solution)/shard_map/all_to_all | solution.py:265
  129.4 37.9 %copy-start.3 = (bf16[512,1024]{1,0:T(8,128)(2,1)S(1)}, bf16[512,1024]{1,0:T(8,128)(2,1)}, u32[]{:S(2)}) copy-start(bf16[512,1024]{1,0:T(8,128)(2,1)} %get-tuple-element.33.values) | copy-start | bytes 3145732
  151.6 22.7 %all-to-all-start.3 = ((bf16[16,64,128]{2,1,0:T(8,128)(2,1)}), bf16[16,64,128]{2,1,0:T(8,128)(2,1)S(1)}, u32[]{:S(2)}, u32[]{:S(2)}) async-start(bf16[16,64,128]{2,1,0:T(8,128)(2,1)} %broadcast_in_dim.5), calls=%async_computation.3 | async-start | bytes 524288 | tf_op jit(solution)/shard_map/all_to_all | solution.py:265
  174.3 32.8 %all-to-all-start.4 = ((bf16[4,512,1024]{2,1,0:T(8,128)(2,1)}), bf16[4,512,1024]{2,1,0:T(8,128)(2,1)}, u32[]{:S(2)}, u32[]{:S(2)}) async-start(bf16[4,512,1024]{2,1,0:T(8,128)(2,1)} %bitcast.50), calls=%async_computation.4 | async-start | bytes 8388608 | tf_op jit(solution)/shard_map/all_to_all | solution.py:321
  180.7 8.3 %copy-start.18 = (bf16[512,512]{1,0:T(8,128)(2,1)S(1)}, bf16[512,512]{1,0:T(8,128)(2,1)}, u32[]{:S(2)}) copy-start(bf16[512,512]{1,0:T(8,128)(2,1)} %copy-done.16) | copy-start | bytes 1572868
  180.7 8.3 %copy-start.21 = (bf16[512,512]{1,0:T(8,128)(2,1)S(1)}, bf16[512,512]{1,0:T(8,128)(2,1)}, u32[]{:S(2)}) copy-start(bf16[512,512]{1,0:T(8,128)(2,1)} %copy-done.19) | copy-start | bytes 1572868
  202.9 46.0 %collective-permute-start.24 = (f32[512,1024]{1,0:T(8,128)}, f32[512,1024]{1,0:T(8,128)}, u32[]{:S(2)}, u32[]{:S(2)}) collective-permute-start(f32[512,1024]{1,0:T(8,128)} %dynamic-slice_bitcast_fusion), channel_id=1, source_target_pairs={{0,1},{1,0},{2,3},{3,2},{4,5},{5,4},{6,7},{7,6},{8,9},{9,8},{10,11... | collective-permute-start | bytes 6291464 | tf_op jit(solution)/shard_map/ppermute | solution.py:358
  235.6 4.3 %collective-permute-start.27 = (bf16[32,1024]{1,0:T(8,128)(2,1)S(1)}, bf16[32,1024]{1,0:T(8,128)(2,1)S(1)}, u32[]{:S(2)}, u32[]{:S(2)}) collective-permute-start(bf16[32,1024]{1,0:T(8,128)(2,1)S(1)} %reduce_sum.52), channel_id=1, source_target_pairs={{0,8},{1,3},{2,10},{3,5},{4,12},{5,7},{6,14},{7,1},{8,16},{9,11},{... | collective-permute-start | bytes 196616 | tf_op jit(solution)/shard_map/ppermute | solution.py:63
  235.6 6.6 %collective-permute-start.26 = (bf16[32,1024]{1,0:T(8,128)(2,1)S(1)}, bf16[32,1024]{1,0:T(8,128)(2,1)S(1)}, u32[]{:S(2)}, u32[]{:S(2)}) collective-permute-start(bf16[32,1024]{1,0:T(8,128)(2,1)S(1)} %reduce_sum.52), channel_id=1, source_target_pairs={{0,16},{1,5},{2,18},{3,7},{4,20},{5,1},{6,22},{7,3},{8,24},{9,13},... | collective-permute-start | bytes 196616 | tf_op jit(solution)/shard_map/ppermute | solution.py:63
  239.1 6.3 %collective-permute-start.25 = (bf16[32,1024]{1,0:T(8,128)(2,1)S(1)}, bf16[32,1024]{1,0:T(8,128)(2,1)S(1)}, u32[]{:S(2)}, u32[]{:S(2)}) collective-permute-start(bf16[32,1024]{1,0:T(8,128)(2,1)S(1)} %reduce_sum.52), channel_id=1, source_target_pairs={{0,24},{1,7},{2,26},{3,1},{4,28},{5,3},{6,30},{7,5},{8,0},{9,15},{... | collective-permute-start | bytes 196616 | tf_op jit(solution)/shard_map/ppermute | solution.py:63
  245.4 13.2 %copy-start = (f32[512,1024]{1,0:T(8,128)S(1)}, f32[512,1024]{1,0:T(8,128)}, u32[]{:S(2)}) copy-start(f32[512,1024]{1,0:T(8,128)} %master.1) | copy-start | bytes 6291460
  245.4 13.2 %copy-start.2 = (f32[512,1024]{1,0:T(8,128)S(1)}, f32[512,1024]{1,0:T(8,128)}, u32[]{:S(2)}) copy-start(f32[512,1024]{1,0:T(8,128)} %moment.1) | copy-start | bytes 6291460
  245.4 9.2 %collective-permute-start.28 = (bf16[128,1024]{1,0:T(8,128)(2,1)S(1)}, bf16[128,1024]{1,0:T(8,128)(2,1)S(1)}, u32[]{:S(2)}, u32[]{:S(2)}) collective-permute-start(bf16[128,1024]{1,0:T(8,128)(2,1)S(1)} %pad_maximum_fusion.2.one), channel_id=1, source_target_pairs={{0,6},{1,25},{2,0},{3,27},{4,2},{5,29},{6,4},{7,31},{8,14},{9,1},{... | collective-permute-start | bytes 786440 | tf_op jit(solution)/shard_map/ppermute | solution.py:63
  247.9 8.0 %collective-permute-start.29 = (bf16[128,1024]{1,0:T(8,128)(2,1)S(1)}, bf16[128,1024]{1,0:T(8,128)(2,1)S(1)}, u32[]{:S(2)}, u32[]{:S(2)}) collective-permute-start(bf16[128,1024]{1,0:T(8,128)(2,1)S(1)} %pad_maximum_fusion.2.one), channel_id=1, source_target_pairs={{0,4},{1,17},{2,6},{3,19},{4,0},{5,21},{6,2},{7,23},{8,12},{9,25},... | collective-permute-start | bytes 786440 | tf_op jit(solution)/shard_map/ppermute | solution.py:63
  248.6 10.0 %collective-permute-start.30 = (bf16[128,1024]{1,0:T(8,128)(2,1)S(1)}, bf16[128,1024]{1,0:T(8,128)(2,1)S(1)}, u32[]{:S(2)}, u32[]{:S(2)}) collective-permute-start(bf16[128,1024]{1,0:T(8,128)(2,1)S(1)} %pad_maximum_fusion.2.one), channel_id=1, source_target_pairs={{0,2},{1,9},{2,4},{3,11},{4,6},{5,13},{6,0},{7,15},{8,10},{9,17},{... | collective-permute-start | bytes 786440 | tf_op jit(solution)/shard_map/ppermute | solution.py:63
  (13 other events, 44.3 us)
